TPU v7x, 256 devices: a whole 4x4x8 slice. The times are simulated.
256 devices in a mesh: img: 32 (over z, x_hi, core), sp: 8 (over x_lo, y).
Axes of the slice: x: 4 (x_hi: 2, x_lo: 2; x = x_hi * 2 + x_lo), y: 4, z: 8, core: 2. Of those that a mesh axis runs over, the one named last changes fastest.
Arguments:
- fresh_qkv: bfloat16 [65536, 9216], P(('img', 'sp')), parts along dimension 0, may hold values from -8 to 8
- stale_kv: bfloat16 [65536, 6144], P(('img', 'sp')), parts along dimension 0, may hold values from -8 to 8
- stale_out: bfloat16 [65536, 3072], P(('img', 'sp')), parts along dimension 0, may hold values from -3 to 3
- edit_count: int32 [256], P(('img', 'sp')), parts along dimension 0, may hold values from 0 to 256, as said below
- edit_rows: int32 [65536], P(('img', 'sp')), parts along dimension 0, may hold values from 0 to 255, as said below
Outputs:
- attention_out: bfloat16 [65536, 3072], P(('img', 'sp')), parts along dimension 0
There are 32 independent parts, one for each index of `img`. A program takes and returns all parts, laid end to end along the dimension named above; each array names one. Nothing has to cross between parts.
Inputs may be any that keep to these rules, and one draw needn't show every extreme that they name: `edit_count`: within each image the counts sum to at most 1536, and one index of sp has exactly 256. `edit_rows`: each block of 256 entries (one index of sp) is a permutation of 0 to 255.
All inputs are finite; a program needn't handle non-finite values.
Results may differ from a plain program's by a relative error of at most 0.004.
Values may be sent and summed in bfloat16 or wider, within the bound.
A program may use at most 192 MiB of HBM per device.

v0:
```python
import jax
import jax.numpy as jnp
from jax import lax
from jax.sharding import PartitionSpec as P

HEADS = 24
HEAD_DIM = 128


def attend(queries, merged):
    rows = queries.shape[0]
    width = queries.shape[1]
    score_scale = HEAD_DIM ** (-0.5)
    query_heads = queries.reshape(rows, HEADS, HEAD_DIM)
    piece = lax.all_gather(merged, "sp", axis=0, tiled=True)
    maxima = jnp.full((HEADS, rows), -jnp.inf, jnp.float32)
    totals = jnp.zeros((HEADS, rows), jnp.float32)
    accum = jnp.zeros((HEADS, rows, HEAD_DIM), jnp.float32)
    key_heads = piece[:, :width].reshape(-1, HEADS, HEAD_DIM)
    value_heads = piece[:, width:].reshape(-1, HEADS, HEAD_DIM)
    scores = (
        jnp.einsum("rhd,khd->hrk", query_heads, key_heads, preferred_element_type=jnp.float32)
        * score_scale
    )
    new_max = jnp.max(scores, axis=2)
    factor = jnp.exp(maxima - new_max)
    weights = jnp.exp(scores - new_max[:, :, None])
    totals = totals * factor + jnp.sum(weights, axis=2)
    update = jnp.einsum(
        "hrk,khd->hrd",
        weights.astype(jnp.bfloat16),
        value_heads,
        preferred_element_type=jnp.float32,
    )
    accum = accum * factor[:, :, None] + update
    maxima, totals, accum = (new_max, totals, accum)
    attended = accum / totals[:, :, None]
    return jnp.transpose(attended, (1, 0, 2)).reshape(rows, width).astype(jnp.bfloat16)


def on_device(fresh_qkv, stale_kv, stale_out, edit_count, edit_rows):
    width = stale_out.shape[1]
    tok_rows = fresh_qkv.shape[0]
    slot_iota = jnp.arange(tok_rows, dtype=jnp.int32)
    own_count = edit_count[0]
    row_slot = jnp.zeros((tok_rows,), jnp.int32).at[edit_rows].set(slot_iota)
    edited = row_slot < own_count
    merged = jnp.where(edited[:, None], fresh_qkv[:, width:], stale_kv)
    queries = fresh_qkv[:, :width]
    fresh_rows = attend(queries, merged)
    return jnp.where(edited[:, None], fresh_rows, stale_out)


def solution(mesh):
    return jax.shard_map(
        on_device,
        mesh=mesh,
        in_specs=(
            P(("img", "sp"), None),
            P(("img", "sp"), None),
            P(("img", "sp"), None),
            P(("img", "sp")),
            P(("img", "sp")),
        ),
        out_specs=P(("img", "sp"), None),
        check_vma=False,
    )
```

profile of v0, /device:TPU:64, one launch (start us, length us, event | category | flops | bytes accessed | tf_op | source)
XLA Modules:
  0.0 367.6 jit_solution(7465443053204934202)
XLA Ops:
  6.5 0.0 slice-start
  6.5 0.0 all-gather.2.cloned.1.call-start
  7.3 0.8 compare_select_fusion
  8.2 4.7 %copy.10 = bf16[256,6144]{0,1:T(8,128)(2,1)} copy(bf16[256,6144]{1,0:T(8,128)(2,1)} %param.6) | data formatting | bytes 6291456 | tf_op args[1]
  12.8 0.0 slice-done
  12.8 2.8 copy.19
  15.7 0.0 slice-start.1
  15.7 1.4 scatter_custom_fusion
  17.1 4.9 %broadcast_select_fusion = bf16[256,6144]{0,1:T(8,128)(2,1)} fusion(bf16[256,6144]{0,1:T(8,128)(2,1)} %copy.19, bf16[256,6144]{0,1:T(8,128)(2,1)} %copy.10, pred[256]{0:T(512)(128)(4,1)S(1)} %broadcast_compare_fusion), kind=kLoop, calls=%fused_computation.12 | loop fusion | flops 1572864 | bytes 9437440 | tf_op jit(solution)/shard_map/jit(_where)/select_n | solution.py:48
  22.0 0.0 all-gather.2.cloned.1.call-update
  22.0 0.0 slice-done.1
  22.0 0.7 copy.20
  22.7 259.5 %all-gather.2.cloned.1.call-done = bf16[2048,6144]{0,1:T(8,128)(2,1)} async-done(((bf16[256,6144]{0,1:T(8,128)(2,1)}), bf16[2048,6144]{0,1:T(8,128)(2,1)}) %all-gather.2.cloned.1.call-update) | async-done | bytes 25165840 | tf_op jit(solution)/shard_map/all_gather | solution.py:15
  282.3 14.0 %fusion.14 = (bf16[2048,3072]{0,1:T(8,128)(2,1)S(1)}, bf16[2048,3072]{0,1:T(8,128)(2,1)}) fusion(bf16[2048,6144]{0,1:T(8,128)(2,1)} %all-gather.2.cloned.1.call-done), kind=kLoop, calls=%fused_computation.21 | loop fusion | bytes 50331648 | tf_op jit(solution)/shard_map/slice | solution.py:19
  296.2 18.1 %bitcast_reduce_fusion = (f32[24,256]{1,0:T(8,128)S(1)}, f32[24,2048,256]{2,1,0:T(8,128)}) fusion(bf16[2048,24,128]{0,2,1:T(8,128)(2,1)S(1)} %bitcast.34, bf16[256,24,128]{0,2,1:T(8,128)(2,1)S(1)} %bitcast.36), kind=kOutput, calls=%fused_computation.2 | convolution fusion | flops 3246385152 | bytes 64512000 | tf_op jit(solution)/shard_map/rhd,khd->hrk/dot_general | solution.py:22
  314.4 19.8 %fusion.1 = f32[24,256]{1,0:T(8,128)S(1)} fusion(f32[24,2048,256]{2,1,0:T(8,128)} %get-tuple-element.8, f32[24,256]{1,0:T(8,128)S(1)} %get-tuple-element.7), kind=kLoop, calls=%fused_computation.4 | loop fusion | flops 37742592 | bytes 50380800 | tf_op jit(solution)/shard_map/reduce_sum | solution.py:28
  334.2 0.0 copy-start
  334.2 23.5 %fusion.8 = bf16[256,24,128]{0,2,1:T(8,128)(2,1)} fusion(bf16[2048,24,128]{0,2,1:T(8,128)(2,1)} %bitcast.35, f32[24,2048,256]{2,1,0:T(8,128)} %get-tuple-element.8, f32[24,256]{1,0:T(8,128)S(1)} %get-tuple-element.7, f32[256,24]{0,1:T(8,128)S(1)} %bitcast_add_fusion.1, f32[256,24]{0,1:T(8,128)S(1)} %multiply_bitcast_fusion), kind=kOutput, calls=%fused_computation.11 | convolution fusion | flops 3261333504 | bytes 64561152 | tf_op jit(solution)/shard_map/hrk,khd->hrd/dot_general | solution.py:29
  357.7 1.7 copy.15
  359.4 0.0 copy-done
  359.4 1.4 broadcast_select_fusion.1
  (4 shorter events, 0.0 us)
Async XLA Ops:
  6.5 6.3 %slice-start = ((bf16[256,9216]{1,0:T(8,128)(2,1)}), bf16[256,6144]{1,0:T(8,128)(2,1)S(1)}, s32[]{:S(2)}) async-start(bf16[256,9216]{1,0:T(8,128)(2,1)} %param.5), calls=%async_computation.1 | async-start | bytes 6291456 | tf_op jit(solution)/shard_map/slice | solution.py:48
  6.5 275.7 %all-gather.2.cloned.1.call-start = ((), (), s32[]{:S(2)}) async-start(), calls=%async_computation | async-start | bytes 28311552 | tf_op jit(solution)/shard_map/all_gather | solution.py:15
  15.7 6.4 %slice-start.1 = ((bf16[256,9216]{1,0:T(8,128)(2,1)}), bf16[256,3072]{1,0:T(8,128)(2,1)S(1)}, s32[]{:S(2)}) async-start(bf16[256,9216]{1,0:T(8,128)(2,1)} %param.5), calls=%async_computation.2 | async-start | bytes 3145728 | tf_op jit(solution)/shard_map/slice | solution.py:49
  334.2 25.2 %copy-start = (bf16[256,3072]{1,0:T(8,128)(2,1)S(1)}, bf16[256,3072]{1,0:T(8,128)(2,1)}, u32[]{:S(2)}) copy-start(bf16[256,3072]{1,0:T(8,128)(2,1)} %param.7) | copy-start | bytes 4718596
Sparse Core Ops, SparseCore 0:
  22.2 260.0 all-gather.1
where the time goes:
time: 369 us; the launch traced here: 368 us
  waiting for transfers between devices  260 us (70%)
  matrix products  41.6 us (11%)
  other arithmetic  27 us (7%)
  local copies, waits for them, and re-layouts  25.3 us (7%)
  between operations  14.3 us (4%)
    all_gather x1, waiting for transfers between devices, attend(): piece = lax.all_gather(merged, 'sp', axis=0, tiled=True)  260 us
    dot_general x1, matrix products, attend(): jnp.einsum('hrk,khd->hrd', weights.astype(jnp.bfloat16), value_heads, pre...  23.5 us
    reduce_sum x1, other arithmetic, attend(): totals = totals * factor + jnp.sum(weights, axis=2)  19.8 us
    dot_general x1, matrix products, attend(): jnp.einsum('rhd,khd->hrk', query_heads, key_heads, preferred_element_type...  18.1 us
    slice x1, local copies, waits for them, and re-layouts, attend(): key_heads = piece[:, :width].reshape(-1, HEADS, HEAD_DIM)  14 us
    unnamed x5, local copies, waits for them, and re-layouts  8.18 us
  transfers between devices with their start and end apart: 1, of which 1 were waited for; matrix products, arithmetic and copies ran while one was open for 0% of the time, Pallas kernels for 0%

commit v1 on v0

v1 whole, which is shorter than its diff:
```python
import functools

import jax
import jax.numpy as jnp
from jax import lax
from jax.experimental import pallas as pl
from jax.experimental.pallas import tpu as pltpu
from jax.sharding import PartitionSpec as P

HEADS = 24
HEAD_DIM = 128
EXP2_SCALE = HEAD_DIM ** (-0.5) * 1.4426950408889634
RING = 4
PEERS = ((1, 0), (0, 1), (0, 3), (1, 2), (1, 1), (1, 3), (0, 2))


def cols(index):
    return pl.ds(pl.multiple_of(index * HEAD_DIM, HEAD_DIM), HEAD_DIM)


def kernel(
    n,
    heads_own,
    count_ref,
    rows_ref,
    fresh,
    stale,
    att,
    mask_ref,
    fresh_kv,
    stale_kv,
    rows_vmem,
    outbox,
    q_all,
    kv_all,
    o_all,
    load_sem,
    q_send,
    q_recv,
    kv_send,
    kv_recv,
    o_send,
    o_recv,
):
    me = lax.axis_index("sp")
    tok = fresh.shape[0]
    width = fresh.shape[1] // 3

    def rows(index):
        return pl.ds(pl.multiple_of(index * tok, tok), tok)

    def peer(step):
        over, along = step
        return lax.rem(me // RING + over, 2) * RING + lax.rem(lax.rem(me, RING) + along, RING)

    rows_load = pltpu.make_async_copy(rows_ref, rows_vmem, load_sem.at[2, 0])
    rows_load.start()
    loads = []
    for part in range(2):
        at = pl.ds(part * width, width)
        loads.append(
            (
                pltpu.make_async_copy(
                    fresh.at[:, pl.ds((part + 1) * width, width)], fresh_kv.at[:, at], load_sem.at[part, 0]
                ),
                pltpu.make_async_copy(stale.at[:, at], stale_kv.at[:, at], load_sem.at[part, 1]),
            )
        )
    for pair in loads:
        for load in pair:
            load.start()

    barrier = pltpu.get_barrier_semaphore()

    for step in PEERS:
        pl.semaphore_signal(
            barrier, inc=1, device_id={"sp": peer(step)}, device_id_type=pl.DeviceIdType.MESH
        )
    pl.semaphore_wait(barrier, n - 1)

    def q_copy(j, dest):
        return pltpu.make_async_remote_copy(
            src_ref=fresh.at[:, cols(dest * heads_own + j)],
            dst_ref=q_all.at[j, rows(me)],
            send_sem=q_send.at[j, dest],
            recv_sem=q_recv.at[j, me],
            device_id={"sp": dest},
            device_id_type=pl.DeviceIdType.MESH,
        )

    def q_own(j):
        return pltpu.make_async_copy(
            fresh.at[:, cols(me * heads_own + j)], q_all.at[j, rows(me)], q_recv.at[j, me]
        )

    def kv_copy(j, dest):
        return pltpu.make_async_remote_copy(
            src_ref=outbox.at[j, dest],
            dst_ref=kv_all.at[j, :, rows(me)],
            send_sem=kv_send.at[j, dest],
            recv_sem=kv_recv.at[j, me],
            device_id={"sp": dest},
            device_id_type=pl.DeviceIdType.MESH,
        )

    def kv_own(j):
        return pltpu.make_async_copy(outbox.at[j, me], kv_all.at[j, :, rows(me)], kv_recv.at[j, me])

    def o_copy(j, dest):
        return pltpu.make_async_remote_copy(
            src_ref=o_all.at[j, rows(dest)],
            dst_ref=att.at[:, cols(me * heads_own + j)],
            send_sem=o_send.at[j, dest],
            recv_sem=o_recv.at[j, me],
            device_id={"sp": dest},
            device_id_type=pl.DeviceIdType.MESH,
        )

    def o_own(j):
        return pltpu.make_async_copy(
            o_all.at[j, rows(me)], att.at[:, cols(me * heads_own + j)], o_recv.at[j, me]
        )

    def send_q(j):
        for step in PEERS:
            q_copy(j, peer(step)).start()
        q_own(j).start()

    def merge(j, dest, mask):
        for part in range(2):
            at = cols(part * HEADS + dest * heads_own + j)
            outbox[j, dest, part] = jnp.where(
                mask, fresh_kv[:, at].astype(jnp.float32), stale_kv[:, at].astype(jnp.float32)
            ).astype(jnp.bfloat16)

    def send_kv(j):
        mask = mask_ref[...] > 0.0
        for step in PEERS:
            merge(j, peer(step), mask)
            kv_copy(j, peer(step)).start()
        merge(j, me, mask)
        kv_own(j).start()

    def wait_q(j, source):
        pltpu.make_async_copy(
            q_all.at[j, rows(source)], q_all.at[j, rows(source)], q_recv.at[j, source]
        ).wait()

    def wait_kv(j, source):
        pltpu.make_async_copy(
            kv_all.at[j, :, rows(source)], kv_all.at[j, :, rows(source)], kv_recv.at[j, source]
        ).wait()

    send_q(0)

    rows_load.wait()
    slot = lax.broadcasted_iota(jnp.int32, (1, tok), 1)
    live = jnp.where(slot < count_ref[0], rows_vmem[...], -1)
    hit = lax.broadcasted_iota(jnp.int32, (tok, tok), 0) == live
    edited = jnp.max(hit.astype(jnp.float32), axis=1, keepdims=True)
    mask_ref[...] = jnp.broadcast_to(edited, (tok, HEAD_DIM))

    for pair in loads:
        for load in pair:
            load.wait()

    send_kv(0)

    def enqueue(j, carry):
        send_kv(j)
        send_q(j)
        return carry

    lax.fori_loop(1, heads_own, enqueue, 0)

    def head(j, carry):
        for step in ((0, 0),) + PEERS:
            wait_kv(j, peer(step))

        def block(index, carry):
            dest = lax.rem(me + index, n)
            wait_q(j, dest)
            scores = lax.dot_general(
                q_all[j, rows(dest)],
                kv_all[j, 0],
                (((1,), (1,)), ((), ())),
                preferred_element_type=jnp.float32,
            )
            top = jnp.max(scores, axis=1, keepdims=True)
            weights = jnp.exp2((scores - top) * EXP2_SCALE)
            total = jnp.sum(weights, axis=1, keepdims=True)
            summed = jnp.dot(
                weights.astype(jnp.bfloat16), kv_all[j, 1], preferred_element_type=jnp.float32
            )
            o_all[j, rows(dest)] = (summed / total).astype(jnp.bfloat16)

            @pl.when(index > 0)
            def _():
                o_copy(j, dest).start()

            @pl.when(index == 0)
            def _():
                o_own(j).start()

            return carry

        lax.fori_loop(0, n, block, 0)
        return carry

    lax.fori_loop(0, heads_own, head, 0)

    def drain(j, carry):
        for step in PEERS:
            q_copy(j, peer(step)).wait_send()
            kv_copy(j, peer(step)).wait_send()
            o_copy(j, peer(step)).wait_send()
        for step in ((0, 0),) + PEERS:
            at = cols(peer(step) * heads_own + j)
            pltpu.make_async_copy(att.at[:, at], att.at[:, at], o_recv.at[j, peer(step)]).wait()
        return carry

    lax.fori_loop(0, heads_own, drain, 0)


def on_device(n, fresh_qkv, stale_kv, stale_out, edit_count, edit_rows):
    tok, width = stale_out.shape
    heads_own = HEADS // n
    total = tok * n
    flops = heads_own * total * total * HEAD_DIM * 4
    bf16 = jnp.bfloat16
    sems = pltpu.SemaphoreType.DMA((heads_own, n))
    att, mask = pl.pallas_call(
        functools.partial(kernel, n, heads_own),
        out_shape=(
            jax.ShapeDtypeStruct((tok, width), bf16),
            jax.ShapeDtypeStruct((tok, HEAD_DIM), jnp.float32),
        ),
        in_specs=[
            pl.BlockSpec(memory_space=pltpu.SMEM),
            pl.BlockSpec(memory_space=pltpu.HBM),
            pl.BlockSpec(memory_space=pltpu.HBM),
            pl.BlockSpec(memory_space=pltpu.HBM),
        ],
        out_specs=(pl.BlockSpec(memory_space=pl.ANY), pl.BlockSpec(memory_space=pltpu.VMEM)),
        scratch_shapes=[
            pltpu.VMEM((tok, 2 * width), bf16),
            pltpu.VMEM((tok, 2 * width), bf16),
            pltpu.VMEM((1, tok), jnp.int32),
            pltpu.VMEM((heads_own, n, 2, tok, HEAD_DIM), bf16),
            pltpu.VMEM((heads_own, total, HEAD_DIM), bf16),
            pltpu.VMEM((heads_own, 2, total, HEAD_DIM), bf16),
            pltpu.VMEM((heads_own, total, HEAD_DIM), bf16),
            pltpu.SemaphoreType.DMA((3, 2)),
            sems,
            sems,
            sems,
            sems,
            sems,
            sems,
        ],
        compiler_params=pltpu.CompilerParams(
            collective_id=0, has_side_effects=True, vmem_limit_bytes=48 * 1024 * 1024
        ),
        cost_estimate=pl.CostEstimate(
            flops=flops, bytes_accessed=8 * tok * width * 2, transcendentals=heads_own * total * total
        ),
    )(
        edit_count,
        pltpu.with_memory_space_constraint(edit_rows.reshape(1, tok), pltpu.HBM),
        pltpu.with_memory_space_constraint(fresh_qkv, pltpu.HBM),
        pltpu.with_memory_space_constraint(stale_kv, pltpu.HBM),
    )
    return jnp.where(mask[:, :1] > 0.0, att, stale_out)


def solution(mesh):
    n = mesh.shape["sp"]
    spec = P(("img", "sp"), None)
    flat = P(("img", "sp"))
    return jax.shard_map(
        functools.partial(on_device, n),
        mesh=mesh,
        in_specs=(spec, spec, spec, flat, flat),
        out_specs=spec,
        check_vma=False,
    )
```

time: 369 us -> 77.9 us (0.21)
  waiting for transfers between devices: 260 us -> 0 us
  Pallas kernels: 0 us -> 75 us
  matrix products: 41.6 us -> 0 us
  other arithmetic: 27 us -> 1.48 us
  local copies, waits for them, and re-layouts: 25.3 us -> 0.01 us
  between operations: 14.3 us -> 0.68 us
    all_gather x1 -> x0, waiting for transfers between devices: 260 us -> none  [attend(): piece = lax.all_gather(merged, 'sp', axis=0, tiled=True)]
    pallas_call x0 -> x1, Pallas kernels: none -> 75 us  [on_device(): pl.pallas_call(functools.partial(kernel, n, heads_own), out_shape=(jax.Sh...]
    dot_general x2 -> x0, matrix products: 41.6 us -> none  [the longest x1 23.5 us: attend(): jnp.einsum('hrk,khd->hrd', weights.astype(jnp.bfloat16), value_heads, pre...]
    reduce_sum x1 -> x0, other arithmetic: 19.8 us -> none  [attend(): totals = totals * factor + jnp.sum(weights, axis=2)]
    slice x5 -> x0, local copies, waits for them, and re-layouts: 14 us -> none  [the longest x1 14 us: attend(): key_heads = piece[:, :width].reshape(-1, HEADS, HEAD_DIM)]
    unnamed x5 -> x2, local copies, waits for them, and re-layouts: 8.18 us -> 0.01 us
    select_n x3 -> x1, other arithmetic: 7.13 us -> 1.37 us  [on_device(): return jnp.where(mask[:, :1] > 0.0, att, stale_out)]
  transfers between devices with their start and end apart: 1 -> 0, of which waited for: 1 -> 0; matrix products, arithmetic and copies ran while one was open for 0% -> 0% of each run, Pallas kernels for 0% -> 0%
where the time goes in v1:
time: 77.9 us; the launch traced here: 77.1 us
  Pallas kernels  75 us (96%)
  other arithmetic  1.48 us (2%)
    pallas_call x1, Pallas kernels, on_device(): pl.pallas_call(functools.partial(kernel, n, heads_own), out_shape=(jax.Sh...  75 us

profile of v1, /device:TPU:64, one launch (start us, length us, event | category | flops | bytes accessed | tf_op | source)
XLA Modules:
  0.0 77.1 jit_solution(17952993392015724686)
XLA Ops:
  0.7 0.0 copy-start
  0.7 75.0 %shard_map.55 = (bf16[256,3072]{1,0:T(8,128)(2,1)S(1)}, f32[256,128]{1,0:T(8,128)S(1)}) custom-call(s32[1]{0:T(128)S(6)} %copy.6.count_ref, s32[1,256]{1,0:T(1,128)} %bitcast.1, bf16[256,9216]{1,0:T(8,128)(2,1)} %fresh.1, bf16[256,6144]{1,0:T(8,128)(2,1)} %stale.1), custom_call_target="tpu_custom_call" | custom-call | flops 6442450944 | bytes 12582912 | tf_op jit(solution)/shard_map/pallas_call | solution.py:232
  75.6 0.1 fusion
  75.7 0.0 copy-done
  75.8 1.4 %broadcast_select_fusion = bf16[256,3072]{1,0:T(8,128)(2,1)} fusion(bf16[256,3072]{1,0:T(8,128)(2,1)S(1)} %get-tuple-element.8, bf16[256,3072]{1,0:T(8,128)(2,1)S(1)} %copy-done, pred[256]{0:T(512)(128)(4,1)S(1)} %fusion), kind=kLoop, calls=%fused_computation | loop fusion | flops 786432 | bytes 4718848 | tf_op jit(solution)/shard_map/jit(_where)/select_n | solution.py:273
Async XLA Ops:
  0.7 75.1 %copy-start = (bf16[256,3072]{1,0:T(8,128)(2,1)S(1)}, bf16[256,3072]{1,0:T(8,128)(2,1)}, u32[]{:S(2)}) copy-start(bf16[256,3072]{1,0:T(8,128)(2,1)} %param.7) | copy-start | bytes 4718596

commit v2 on v1

--- a/solution.py
+++ b/solution.py
@@ -11,7 +11,9 @@
 HEAD_DIM = 128
 EXP2_SCALE = HEAD_DIM ** (-0.5) * 1.4426950408889634
 RING = 4
-PEERS = ((1, 0), (0, 1), (0, 3), (1, 2), (1, 1), (1, 3), (0, 2))
+BLOCKS = 4
+CHUNK = 16
+PEERS = ((1, 2), (0, 2), (1, 1), (1, 3), (0, 1), (0, 3), (1, 0))
 
 
 def cols(index):
@@ -25,6 +27,8 @@
     rows_ref,
     fresh,
     stale,
+    stale_out,
+    out_ref,
     att,
     mask_ref,
     fresh_kv,
@@ -34,6 +38,8 @@
     q_all,
     kv_all,
     o_all,
+    scores,
+    probs,
     load_sem,
     q_send,
     q_recv,
@@ -49,12 +55,15 @@
     def rows(index):
         return pl.ds(pl.multiple_of(index * tok, tok), tok)
 
+    turn_of = 1 + 2 * lax.rem(lax.axis_index("img"), 2)
+
     def peer(step):
         over, along = step
-        return lax.rem(me // RING + over, 2) * RING + lax.rem(lax.rem(me, RING) + along, RING)
+        return lax.rem(me // RING + over, 2) * RING + lax.rem(lax.rem(me, RING) + along * turn_of, RING)
 
     rows_load = pltpu.make_async_copy(rows_ref, rows_vmem, load_sem.at[2, 0])
     rows_load.start()
+    out_load = pltpu.make_async_copy(stale_out, out_ref, load_sem.at[2, 1])
     loads = []
     for part in range(2):
         at = pl.ds(part * width, width)
@@ -164,59 +173,110 @@
         for load in pair:
             load.wait()
 
+    def sent_q(j):
+        for step in PEERS:
+            q_copy(j, peer(step)).wait_send()
+
+    def sent_kv(j):
+        for step in PEERS:
+            kv_copy(j, peer(step)).wait_send()
+
+    out_load.start()
     send_kv(0)
-
-    def enqueue(j, carry):
-        send_kv(j)
-        send_q(j)
+    sent_q(0)
+    send_kv(1)
+    sent_kv(0)
+    send_q(1)
+
+    def score(j, dest, slot):
+        scores[slot] = lax.dot_general(
+            q_all[j, rows(dest)],
+            kv_all[j, 0],
+            (((1,), (1,)), ((), ())),
+            preferred_element_type=jnp.float32,
+        )
+
+    def soften(slot):
+        for first in range(0, tok, CHUNK):
+            piece = scores[slot, first : first + CHUNK]
+            top = jnp.max(piece, axis=1, keepdims=True)
+            probs[slot, first : first + CHUNK] = jnp.exp2((piece - top) * EXP2_SCALE).astype(jnp.bfloat16)
+
+    def gather(j, dest, slot):
+        values = kv_all[j, 1]
+        summed = jnp.dot(
+            probs[slot],
+            jnp.concatenate([values, jnp.ones_like(values)], axis=1),
+            preferred_element_type=jnp.float32,
+        )
+        o_all[j, rows(dest)] = (summed[:, :HEAD_DIM] / summed[:, HEAD_DIM:]).astype(jnp.bfloat16)
+
+    order = PEERS + ((0, 0),)
+
+    def send_o(j, step):
+        if step == (0, 0):
+            o_own(j).start()
+        else:
+            o_copy(j, peer(step)).start()
+
+    def head(j, carry):
+        @pl.when(j > 0)
+        def _():
+            sent_kv(j)
+
+            @pl.when(j + 1 < heads_own)
+            def _():
+                send_kv(j + 1)
+
+            sent_q(j)
+
+            @pl.when(j + 1 < heads_own)
+            def _():
+                send_q(j + 1)
+
+        @pl.when(j + 1 == heads_own)
+        def _():
+            def early(before, carry):
+                for step in order:
+                    send_o(before, step)
+                return carry
+
+            lax.fori_loop(0, heads_own - 1, early, 0)
+
+        for step in order:
+            wait_kv(j, peer(step))
+            wait_q(j, peer(step))
+
+        for first in range(0, n, BLOCKS):
+            steps = order[first : first + BLOCKS]
+            score(j, peer(steps[0]), 0)
+            for index, step in enumerate(steps):
+                if index + 1 < BLOCKS:
+                    score(j, peer(steps[index + 1]), (index + 1) % 2)
+                soften(index % 2)
+                gather(j, peer(step), index % 2)
+
+            @pl.when(j + 1 == heads_own)
+            def _():
+                for step in steps:
+                    send_o(j, step)
+
         return carry
 
-    lax.fori_loop(1, heads_own, enqueue, 0)
-
-    def head(j, carry):
-        for step in ((0, 0),) + PEERS:
-            wait_kv(j, peer(step))
-
-        def block(index, carry):
-            dest = lax.rem(me + index, n)
-            wait_q(j, dest)
-            scores = lax.dot_general(
-                q_all[j, rows(dest)],
-                kv_all[j, 0],
-                (((1,), (1,)), ((), ())),
-                preferred_element_type=jnp.float32,
-            )
-            top = jnp.max(scores, axis=1, keepdims=True)
-            weights = jnp.exp2((scores - top) * EXP2_SCALE)
-            total = jnp.sum(weights, axis=1, keepdims=True)
-            summed = jnp.dot(
-                weights.astype(jnp.bfloat16), kv_all[j, 1], preferred_element_type=jnp.float32
-            )
-            o_all[j, rows(dest)] = (summed / total).astype(jnp.bfloat16)
-
-            @pl.when(index > 0)
-            def _():
-                o_copy(j, dest).start()
-
-            @pl.when(index == 0)
-            def _():
-                o_own(j).start()
-
-            return carry
-
-        lax.fori_loop(0, n, block, 0)
-        return carry
-
     lax.fori_loop(0, heads_own, head, 0)
 
+    out_load.wait()
+
     def drain(j, carry):
-        for step in PEERS:
-            q_copy(j, peer(step)).wait_send()
-            kv_copy(j, peer(step)).wait_send()
-            o_copy(j, peer(step)).wait_send()
-        for step in ((0, 0),) + PEERS:
+        mask = mask_ref[...] > 0.0
+        for step in PEERS[::-1] + ((0, 0),):
             at = cols(peer(step) * heads_own + j)
             pltpu.make_async_copy(att.at[:, at], att.at[:, at], o_recv.at[j, peer(step)]).wait()
+            out_ref[:, at] = jnp.where(
+                mask, att[:, at].astype(jnp.float32), out_ref[:, at].astype(jnp.float32)
+            ).astype(jnp.bfloat16)
+        for step in PEERS:
+            o_copy(j, peer(step)).wait_send()
         return carry
 
     lax.fori_loop(0, heads_own, drain, 0)
@@ -229,20 +289,20 @@
     flops = heads_own * total * total * HEAD_DIM * 4
     bf16 = jnp.bfloat16
     sems = pltpu.SemaphoreType.DMA((heads_own, n))
-    att, mask = pl.pallas_call(
+    return pl.pallas_call(
         functools.partial(kernel, n, heads_own),
-        out_shape=(
-            jax.ShapeDtypeStruct((tok, width), bf16),
-            jax.ShapeDtypeStruct((tok, HEAD_DIM), jnp.float32),
-        ),
+        out_shape=jax.ShapeDtypeStruct((tok, width), bf16),
         in_specs=[
             pl.BlockSpec(memory_space=pltpu.SMEM),
             pl.BlockSpec(memory_space=pltpu.HBM),
             pl.BlockSpec(memory_space=pltpu.HBM),
             pl.BlockSpec(memory_space=pltpu.HBM),
+            pl.BlockSpec(memory_space=pltpu.HBM),
         ],
-        out_specs=(pl.BlockSpec(memory_space=pl.ANY), pl.BlockSpec(memory_space=pltpu.VMEM)),
+        out_specs=pl.BlockSpec(memory_space=pltpu.VMEM),
         scratch_shapes=[
+            pltpu.VMEM((tok, width), bf16),
+            pltpu.VMEM((tok, HEAD_DIM), jnp.float32),
             pltpu.VMEM((tok, 2 * width), bf16),
             pltpu.VMEM((tok, 2 * width), bf16),
             pltpu.VMEM((1, tok), jnp.int32),
@@ -250,6 +310,8 @@
             pltpu.VMEM((heads_own, total, HEAD_DIM), bf16),
             pltpu.VMEM((heads_own, 2, total, HEAD_DIM), bf16),
             pltpu.VMEM((heads_own, total, HEAD_DIM), bf16),
+            pltpu.VMEM((2, tok, total), jnp.float32),
+            pltpu.VMEM((2, tok, total), bf16),
             pltpu.SemaphoreType.DMA((3, 2)),
             sems,
             sems,
@@ -269,8 +331,8 @@
         pltpu.with_memory_space_constraint(edit_rows.reshape(1, tok), pltpu.HBM),
         pltpu.with_memory_space_constraint(fresh_qkv, pltpu.HBM),
         pltpu.with_memory_space_constraint(stale_kv, pltpu.HBM),
+        pltpu.with_memory_space_constraint(stale_out, pltpu.HBM),
     )
-    return jnp.where(mask[:, :1] > 0.0, att, stale_out)
 
 
 def solution(mesh):

time: 77.9 us -> 76.9 us (0.987)
  other arithmetic: 1.48 us -> 0 us
  local copies, waits for them, and re-layouts: 0.01 us -> 1.15 us
    select_n x1 -> x0, other arithmetic: 1.37 us -> none  [on_device(): return jnp.where(mask[:, :1] > 0.0, att, stale_out)]
    unnamed x2 -> x1, local copies, waits for them, and re-layouts: 0.01 us -> 1.15 us
where the time goes in v2:
time: 76.9 us; the launch traced here: 76.8 us
  Pallas kernels  75 us (98%)
  local copies, waits for them, and re-layouts  1.15 us (1%)
    pallas_call x1, Pallas kernels, on_device(): pl.pallas_call(functools.partial(kernel, n, heads_own), out_shape=jax.Sha...  75 us

profile of v2, /device:TPU:64, one launch (start us, length us, event | category | flops | bytes accessed | tf_op | source)
XLA Modules:
  0.0 76.8 jit_solution(9389807680199293038)
XLA Ops:
  0.7 75.0 %shard_map.55 = bf16[256,3072]{1,0:T(8,128)(2,1)S(1)} custom-call(s32[1]{0:T(128)S(6)} %copy.7.count_ref, s32[1,256]{1,0:T(1,128)} %bitcast.1, bf16[256,9216]{1,0:T(8,128)(2,1)} %fresh.1, bf16[256,6144]{1,0:T(8,128)(2,1)} %stale.1, bf16[256,3072]{1,0:T(8,128)(2,1)} %stale_out.1), custom_call_target="tpu_custom_call" | custom-call | flops 6442450944 | bytes 12582912 | tf_op jit(solution)/shard_map/pallas_call | solution.py:292
  75.6 1.1 %copy.8 = bf16[256,3072]{1,0:T(8,128)(2,1)} copy(bf16[256,3072]{1,0:T(8,128)(2,1)S(1)} %shard_map.55) | data formatting | bytes 3145728

commit v3 on v2

--- a/solution.py
+++ b/solution.py
@@ -61,6 +61,12 @@
         over, along = step
         return lax.rem(me // RING + over, 2) * RING + lax.rem(lax.rem(me, RING) + along * turn_of, RING)
 
+    barrier = pltpu.get_barrier_semaphore()
+
+    for step in PEERS:
+        pl.semaphore_signal(
+            barrier, inc=1, device_id={"sp": peer(step)}, device_id_type=pl.DeviceIdType.MESH
+        )
     rows_load = pltpu.make_async_copy(rows_ref, rows_vmem, load_sem.at[2, 0])
     rows_load.start()
     out_load = pltpu.make_async_copy(stale_out, out_ref, load_sem.at[2, 1])
@@ -79,12 +85,6 @@
         for load in pair:
             load.start()
 
-    barrier = pltpu.get_barrier_semaphore()
-
-    for step in PEERS:
-        pl.semaphore_signal(
-            barrier, inc=1, device_id={"sp": peer(step)}, device_id_type=pl.DeviceIdType.MESH
-        )
     pl.semaphore_wait(barrier, n - 1)
 
     def q_copy(j, dest):
@@ -183,10 +183,13 @@
 
     out_load.start()
     send_kv(0)
-    sent_q(0)
-    send_kv(1)
-    sent_kv(0)
-    send_q(1)
+
+    def enqueue(j, carry):
+        send_kv(j)
+        send_q(j)
+        return carry
+
+    lax.fori_loop(1, heads_own, enqueue, 0)
 
     def score(j, dest, slot):
         scores[slot] = lax.dot_general(
@@ -219,30 +222,7 @@
         else:
             o_copy(j, peer(step)).start()
 
-    def head(j, carry):
-        @pl.when(j > 0)
-        def _():
-            sent_kv(j)
-
-            @pl.when(j + 1 < heads_own)
-            def _():
-                send_kv(j + 1)
-
-            sent_q(j)
-
-            @pl.when(j + 1 < heads_own)
-            def _():
-                send_q(j + 1)
-
-        @pl.when(j + 1 == heads_own)
-        def _():
-            def early(before, carry):
-                for step in order:
-                    send_o(before, step)
-                return carry
-
-            lax.fori_loop(0, heads_own - 1, early, 0)
-
+    def head(j, carry, last=False):
         for step in order:
             wait_kv(j, peer(step))
             wait_q(j, peer(step))
@@ -255,15 +235,29 @@
                     score(j, peer(steps[index + 1]), (index + 1) % 2)
                 soften(index % 2)
                 gather(j, peer(step), index % 2)
-
-            @pl.when(j + 1 == heads_own)
-            def _():
-                for step in steps:
+                if last:
                     send_o(j, step)
 
         return carry
 
-    lax.fori_loop(0, heads_own, head, 0)
+    def outputs(j, carry):
+        for step in order:
+            send_o(j, step)
+        return carry
+
+    def sent(j, carry):
+        sent_kv(j)
+        sent_q(j)
+        return carry
+
+    final = heads_own - 1
+    lax.fori_loop(0, final, head, 0)
+    lax.fori_loop(0, final, sent, 0)
+    sent_kv(final)
+    lax.fori_loop(0, final - 1, outputs, 0)
+    sent_q(final)
+    outputs(final - 1, 0)
+    head(final, 0, last=True)
 
     out_load.wait()
 

time: 76.9 us -> 77.6 us (level)
  no operation moved by 1% of the time
where the time goes in v3:
time: 77.6 us; the launch traced here: 76.8 us
  Pallas kernels  75 us (97%)
  local copies, waits for them, and re-layouts  1.15 us (1%)
    pallas_call x1, Pallas kernels, on_device(): pl.pallas_call(functools.partial(kernel, n, heads_own), out_shape=jax.Sha...  75 us

profile of v3, /device:TPU:64, one launch (start us, length us, event | category | flops | bytes accessed | tf_op | source)
XLA Modules:
  0.0 76.8 jit_solution(13417767164157868912)
XLA Ops:
  0.7 75.0 %shard_map.55 = bf16[256,3072]{1,0:T(8,128)(2,1)S(1)} custom-call(s32[1]{0:T(128)S(6)} %copy.7.count_ref, s32[1,256]{1,0:T(1,128)} %bitcast.1, bf16[256,9216]{1,0:T(8,128)(2,1)} %fresh.1, bf16[256,6144]{1,0:T(8,128)(2,1)} %stale.1, bf16[256,3072]{1,0:T(8,128)(2,1)} %stale_out.1), custom_call_target="tpu_custom_call" | custom-call | flops 6442450944 | bytes 12582912 | tf_op jit(solution)/shard_map/pallas_call | solution.py:286
  75.6 1.1 %copy.8 = bf16[256,3072]{1,0:T(8,128)(2,1)} copy(bf16[256,3072]{1,0:T(8,128)(2,1)S(1)} %shard_map.55) | data formatting | bytes 3145728

commit v4 on v2

--- a/solution.py
+++ b/solution.py
@@ -34,6 +34,8 @@
     fresh_kv,
     stale_kv,
     rows_vmem,
+    q_box,
+    stage_sem,
     outbox,
     q_all,
     kv_all,
@@ -61,6 +63,12 @@
         over, along = step
         return lax.rem(me // RING + over, 2) * RING + lax.rem(lax.rem(me, RING) + along * turn_of, RING)
 
+    barrier = pltpu.get_barrier_semaphore()
+
+    for step in PEERS:
+        pl.semaphore_signal(
+            barrier, inc=1, device_id={"sp": peer(step)}, device_id_type=pl.DeviceIdType.MESH
+        )
     rows_load = pltpu.make_async_copy(rows_ref, rows_vmem, load_sem.at[2, 0])
     rows_load.start()
     out_load = pltpu.make_async_copy(stale_out, out_ref, load_sem.at[2, 1])
@@ -75,21 +83,16 @@
                 pltpu.make_async_copy(stale.at[:, at], stale_kv.at[:, at], load_sem.at[part, 1]),
             )
         )
-    for pair in loads:
-        for load in pair:
-            load.start()
-
-    barrier = pltpu.get_barrier_semaphore()
-
-    for step in PEERS:
-        pl.semaphore_signal(
-            barrier, inc=1, device_id={"sp": peer(step)}, device_id_type=pl.DeviceIdType.MESH
-        )
     pl.semaphore_wait(barrier, n - 1)
+
+    def q_source(j, dest):
+        if isinstance(j, int) and j == 0:
+            return fresh.at[:, cols(dest * heads_own)]
+        return q_box.at[j - 1, dest]
 
     def q_copy(j, dest):
         return pltpu.make_async_remote_copy(
-            src_ref=fresh.at[:, cols(dest * heads_own + j)],
+            src_ref=q_source(j, dest),
             dst_ref=q_all.at[j, rows(me)],
             send_sem=q_send.at[j, dest],
             recv_sem=q_recv.at[j, me],
@@ -98,9 +101,7 @@
         )
 
     def q_own(j):
-        return pltpu.make_async_copy(
-            fresh.at[:, cols(me * heads_own + j)], q_all.at[j, rows(me)], q_recv.at[j, me]
-        )
+        return pltpu.make_async_copy(q_source(j, me), q_all.at[j, rows(me)], q_recv.at[j, me])
 
     def kv_copy(j, dest):
         return pltpu.make_async_remote_copy(
@@ -118,7 +119,7 @@
     def o_copy(j, dest):
         return pltpu.make_async_remote_copy(
             src_ref=o_all.at[j, rows(dest)],
-            dst_ref=att.at[:, cols(me * heads_own + j)],
+            dst_ref=att.at[me * heads_own + j],
             send_sem=o_send.at[j, dest],
             recv_sem=o_recv.at[j, me],
             device_id={"sp": dest},
@@ -127,7 +128,7 @@
 
     def o_own(j):
         return pltpu.make_async_copy(
-            o_all.at[j, rows(me)], att.at[:, cols(me * heads_own + j)], o_recv.at[j, me]
+            o_all.at[j, rows(me)], att.at[me * heads_own + j], o_recv.at[j, me]
         )
 
     def send_q(j):
@@ -161,6 +162,16 @@
         ).wait()
 
     send_q(0)
+    for pair in loads:
+        for load in pair:
+            load.start()
+    stages = [
+        pltpu.make_async_copy(fresh.at[:, cols(dest * heads_own + j)], q_box.at[j - 1, dest], stage_sem.at[j - 1, dest])
+        for j in range(1, heads_own)
+        for dest in range(n)
+    ]
+    for stage in stages:
+        stage.start()
 
     rows_load.wait()
     slot = lax.broadcasted_iota(jnp.int32, (1, tok), 1)
@@ -184,6 +195,8 @@
     out_load.start()
     send_kv(0)
     sent_q(0)
+    for stage in stages:
+        stage.wait()
     send_kv(1)
     sent_kv(0)
     send_q(1)
@@ -270,10 +283,11 @@
     def drain(j, carry):
         mask = mask_ref[...] > 0.0
         for step in PEERS[::-1] + ((0, 0),):
-            at = cols(peer(step) * heads_own + j)
-            pltpu.make_async_copy(att.at[:, at], att.at[:, at], o_recv.at[j, peer(step)]).wait()
+            index = peer(step) * heads_own + j
+            at = cols(index)
+            pltpu.make_async_copy(att.at[index], att.at[index], o_recv.at[j, peer(step)]).wait()
             out_ref[:, at] = jnp.where(
-                mask, att[:, at].astype(jnp.float32), out_ref[:, at].astype(jnp.float32)
+                mask, att[index].astype(jnp.float32), out_ref[:, at].astype(jnp.float32)
             ).astype(jnp.bfloat16)
         for step in PEERS:
             o_copy(j, peer(step)).wait_send()
@@ -301,11 +315,13 @@
         ],
         out_specs=pl.BlockSpec(memory_space=pltpu.VMEM),
         scratch_shapes=[
-            pltpu.VMEM((tok, width), bf16),
+            pltpu.VMEM((HEADS, tok, HEAD_DIM), bf16),
             pltpu.VMEM((tok, HEAD_DIM), jnp.float32),
             pltpu.VMEM((tok, 2 * width), bf16),
             pltpu.VMEM((tok, 2 * width), bf16),
             pltpu.VMEM((1, tok), jnp.int32),
+            pltpu.VMEM((heads_own - 1, n, tok, HEAD_DIM), bf16),
+            pltpu.SemaphoreType.DMA((heads_own - 1, n)),
             pltpu.VMEM((heads_own, n, 2, tok, HEAD_DIM), bf16),
             pltpu.VMEM((heads_own, total, HEAD_DIM), bf16),
             pltpu.VMEM((heads_own, 2, total, HEAD_DIM), bf16),

time: 76.9 us -> 76.9 us (level)
  no operation moved by 1% of the time
where the time goes in v4:
time: 76.9 us
  Pallas kernels  75 us (98%)
  local copies, waits for them, and re-layouts  1.15 us (1%)
    pallas_call x1, Pallas kernels, on_device(): pl.pallas_call(functools.partial(kernel, n, heads_own), out_shape=jax.Sha...  75 us

profile of v4, /device:TPU:64, one launch (start us, length us, event | category | flops | bytes accessed | tf_op | source)
XLA Modules:
  0.0 76.9 jit_solution(14749811801700698238)
XLA Ops:
  0.7 75.0 %shard_map.55 = bf16[256,3072]{1,0:T(8,128)(2,1)S(1)} custom-call(s32[1]{0:T(128)S(6)} %copy.7.count_ref, s32[1,256]{1,0:T(1,128)} %bitcast.1, bf16[256,9216]{1,0:T(8,128)(2,1)} %fresh.1, bf16[256,6144]{1,0:T(8,128)(2,1)} %stale.1, bf16[256,3072]{1,0:T(8,128)(2,1)} %stale_out.1), custom_call_target="tpu_custom_call" | custom-call | flops 6442450944 | bytes 12582912 | tf_op jit(solution)/shard_map/pallas_call | solution.py:306
  75.7 1.1 %copy.8 = bf16[256,3072]{1,0:T(8,128)(2,1)} copy(bf16[256,3072]{1,0:T(8,128)(2,1)S(1)} %shard_map.55) | data formatting | bytes 3145728

commit v5 on v4

--- a/solution.py
+++ b/solution.py
@@ -13,7 +13,11 @@
 RING = 4
 BLOCKS = 4
 CHUNK = 16
-PEERS = ((1, 2), (0, 2), (1, 1), (1, 3), (0, 1), (0, 3), (1, 0))
+SLABS = 8
+ORDERS = (
+    ((1, 2), (0, 2), (1, 1), (0, 1), (1, 3), (0, 3), (1, 0)),
+    ((0, 2), (1, 2), (0, 3), (1, 3), (0, 1), (1, 1), (1, 0)),
+)
 
 
 def cols(index):
@@ -57,18 +61,17 @@
     def rows(index):
         return pl.ds(pl.multiple_of(index * tok, tok), tok)
 
-    turn_of = 1 + 2 * lax.rem(lax.axis_index("img"), 2)
-
-    def peer(step):
+    def device_at(step):
         over, along = step
-        return lax.rem(me // RING + over, 2) * RING + lax.rem(lax.rem(me, RING) + along * turn_of, RING)
+        return lax.rem(me // RING + over, 2) * RING + lax.rem(lax.rem(me, RING) + along, RING)
+
+    first_core = lax.rem(lax.axis_index("img"), 2) == 0
+    peers = [jnp.where(first_core, device_at(one), device_at(other)) for one, other in zip(*ORDERS)]
 
     barrier = pltpu.get_barrier_semaphore()
 
-    for step in PEERS:
-        pl.semaphore_signal(
-            barrier, inc=1, device_id={"sp": peer(step)}, device_id_type=pl.DeviceIdType.MESH
-        )
+    for dest in peers:
+        pl.semaphore_signal(barrier, inc=1, device_id={"sp": dest}, device_id_type=pl.DeviceIdType.MESH)
     rows_load = pltpu.make_async_copy(rows_ref, rows_vmem, load_sem.at[2, 0])
     rows_load.start()
     out_load = pltpu.make_async_copy(stale_out, out_ref, load_sem.at[2, 1])
@@ -132,8 +135,8 @@
         )
 
     def send_q(j):
-        for step in PEERS:
-            q_copy(j, peer(step)).start()
+        for dest in peers:
+            q_copy(j, dest).start()
         q_own(j).start()
 
     def merge(j, dest, mask):
@@ -145,9 +148,9 @@
 
     def send_kv(j):
         mask = mask_ref[...] > 0.0
-        for step in PEERS:
-            merge(j, peer(step), mask)
-            kv_copy(j, peer(step)).start()
+        for dest in peers:
+            merge(j, dest, mask)
+            kv_copy(j, dest).start()
         merge(j, me, mask)
         kv_own(j).start()
 
@@ -185,12 +188,12 @@
             load.wait()
 
     def sent_q(j):
-        for step in PEERS:
-            q_copy(j, peer(step)).wait_send()
+        for dest in peers:
+            q_copy(j, dest).wait_send()
 
     def sent_kv(j):
-        for step in PEERS:
-            kv_copy(j, peer(step)).wait_send()
+        for dest in peers:
+            kv_copy(j, dest).wait_send()
 
     out_load.start()
     send_kv(0)
@@ -224,13 +227,13 @@
         )
         o_all[j, rows(dest)] = (summed[:, :HEAD_DIM] / summed[:, HEAD_DIM:]).astype(jnp.bfloat16)
 
-    order = PEERS + ((0, 0),)
-
-    def send_o(j, step):
-        if step == (0, 0):
+    order = peers + [me]
+
+    def send_o(j, dest):
+        if dest is me:
             o_own(j).start()
         else:
-            o_copy(j, peer(step)).start()
+            o_copy(j, dest).start()
 
     def head(j, carry):
         @pl.when(j > 0)
@@ -250,29 +253,30 @@
         @pl.when(j + 1 == heads_own)
         def _():
             def early(before, carry):
-                for step in order:
-                    send_o(before, step)
+                for dest in order:
+                    send_o(before, dest)
                 return carry
 
             lax.fori_loop(0, heads_own - 1, early, 0)
 
-        for step in order:
-            wait_kv(j, peer(step))
-            wait_q(j, peer(step))
+        for dest in order:
+            wait_kv(j, dest)
 
         for first in range(0, n, BLOCKS):
-            steps = order[first : first + BLOCKS]
-            score(j, peer(steps[0]), 0)
-            for index, step in enumerate(steps):
+            dests = order[first : first + BLOCKS]
+            for dest in dests:
+                wait_q(j, dest)
+            score(j, dests[0], 0)
+            for index, dest in enumerate(dests):
                 if index + 1 < BLOCKS:
-                    score(j, peer(steps[index + 1]), (index + 1) % 2)
+                    score(j, dests[index + 1], (index + 1) % 2)
                 soften(index % 2)
-                gather(j, peer(step), index % 2)
+                gather(j, dest, index % 2)
 
             @pl.when(j + 1 == heads_own)
             def _():
-                for step in steps:
-                    send_o(j, step)
+                for dest in dests:
+                    send_o(j, dest)
 
         return carry
 
@@ -282,18 +286,30 @@
 
     def drain(j, carry):
         mask = mask_ref[...] > 0.0
-        for step in PEERS[::-1] + ((0, 0),):
-            index = peer(step) * heads_own + j
+        for source in peers[::-1] + [me]:
+            index = source * heads_own + j
             at = cols(index)
-            pltpu.make_async_copy(att.at[index], att.at[index], o_recv.at[j, peer(step)]).wait()
+            pltpu.make_async_copy(att.at[index], att.at[index], o_recv.at[j, source]).wait()
             out_ref[:, at] = jnp.where(
                 mask, att[index].astype(jnp.float32), out_ref[:, at].astype(jnp.float32)
             ).astype(jnp.bfloat16)
-        for step in PEERS:
-            o_copy(j, peer(step)).wait_send()
+        for dest in peers:
+            o_copy(j, dest).wait_send()
         return carry
 
     lax.fori_loop(0, heads_own, drain, 0)
+
+
+def settle(merged, out, sems):
+    slab = merged.shape[0] // SLABS
+    copies = [
+        pltpu.make_async_copy(merged.at[pl.ds(at * slab, slab)], out.at[pl.ds(at * slab, slab)], sems.at[at])
+        for at in range(SLABS)
+    ]
+    for copy in copies:
+        copy.start()
+    for copy in copies:
+        copy.wait()
 
 
 def on_device(n, fresh_qkv, stale_kv, stale_out, edit_count, edit_rows):
@@ -303,7 +319,7 @@
     flops = heads_own * total * total * HEAD_DIM * 4
     bf16 = jnp.bfloat16
     sems = pltpu.SemaphoreType.DMA((heads_own, n))
-    return pl.pallas_call(
+    merged = pl.pallas_call(
         functools.partial(kernel, n, heads_own),
         out_shape=jax.ShapeDtypeStruct((tok, width), bf16),
         in_specs=[
@@ -349,6 +365,14 @@
         pltpu.with_memory_space_constraint(stale_kv, pltpu.HBM),
         pltpu.with_memory_space_constraint(stale_out, pltpu.HBM),
     )
+    return pl.pallas_call(
+        settle,
+        out_shape=jax.ShapeDtypeStruct((tok, width), bf16),
+        in_specs=[pl.BlockSpec(memory_space=pltpu.VMEM)],
+        out_specs=pl.BlockSpec(memory_space=pltpu.HBM),
+        scratch_shapes=[pltpu.SemaphoreType.DMA((SLABS,))],
+        cost_estimate=pl.CostEstimate(flops=0, bytes_accessed=2 * tok * width, transcendentals=0),
+    )(pltpu.with_memory_space_constraint(merged, pltpu.VMEM))
 
 
 def solution(mesh):

time: 76.9 us -> 77 us (level)
  Pallas kernels: 75 us -> 76.3 us
  local copies, waits for them, and re-layouts: 1.15 us -> 0 us
    pallas_call x0 -> x1, Pallas kernels: none -> 1.2 us  [on_device(): pl.pallas_call(settle, out_shape=jax.ShapeDtypeStruct((tok, width), bf16)...]
    unnamed x1 -> x0, local copies, waits for them, and re-layouts: 1.15 us -> none
where the time goes in v5:
time: 77 us; the launch traced here: 76.9 us
  Pallas kernels  76.3 us (99%)
    pallas_call x1, Pallas kernels, on_device(): pl.pallas_call(functools.partial(kernel, n, heads_own), out_shape=jax.Sha...  75.1 us

profile of v5, /device:TPU:64, one launch (start us, length us, event | category | flops | bytes accessed | tf_op | source)
XLA Modules:
  0.0 76.9 jit_solution(3763326938240753696)
XLA Ops:
  0.7 75.1 %shard_map.55.merged = bf16[256,3072]{1,0:T(8,128)(2,1)S(1)} custom-call(s32[1]{0:T(128)S(6)} %copy.6.count_ref, s32[1,256]{1,0:T(1,128)} %bitcast.1, bf16[256,9216]{1,0:T(8,128)(2,1)} %fresh.1, bf16[256,6144]{1,0:T(8,128)(2,1)} %stale.1, bf16[256,3072]{1,0:T(8,128)(2,1)} %stale_out.1), custom_call_target="tpu_custom_call" | custom-call | flops 6442450944 | bytes 12582912 | tf_op jit(solution)/shard_map/pallas_call | solution.py:322
  75.7 1.2 %shard_map.56 = bf16[256,3072]{1,0:T(8,128)(2,1)} custom-call(bf16[256,3072]{1,0:T(8,128)(2,1)S(1)} %shard_map.55.merged), custom_call_target="tpu_custom_call" | custom-call | bytes 1572864 | tf_op jit(solution)/shard_map/pallas_call | solution.py:368

commit v6 on v4

--- a/solution.py
+++ b/solution.py
@@ -201,6 +201,13 @@
     sent_kv(0)
     send_q(1)
 
+    first_core = turn_of == 1
+
+    @pl.when(first_core)
+    def _():
+        send_kv(heads_own - 1)
+        send_q(heads_own - 1)
+
     def score(j, dest, slot):
         scores[slot] = lax.dot_general(
             q_all[j, rows(dest)],
@@ -237,13 +244,13 @@
         def _():
             sent_kv(j)
 
-            @pl.when(j + 1 < heads_own)
+            @pl.when(jnp.logical_and(j + 1 < heads_own, jnp.logical_not(first_core)))
             def _():
                 send_kv(j + 1)
 
             sent_q(j)
 
-            @pl.when(j + 1 < heads_own)
+            @pl.when(jnp.logical_and(j + 1 < heads_own, jnp.logical_not(first_core)))
             def _():
                 send_q(j + 1)
 

time: 76.9 us -> 76.9 us (level)
  no operation moved by 1% of the time
where the time goes in v6:
time: 76.9 us
  Pallas kernels  75 us (98%)
  local copies, waits for them, and re-layouts  1.15 us (1%)
    pallas_call x1, Pallas kernels, on_device(): pl.pallas_call(functools.partial(kernel, n, heads_own), out_shape=jax.Sha...  75 us

profile of v6, /device:TPU:64, one launch (start us, length us, event | category | flops | bytes accessed | tf_op | source)
XLA Modules:
  0.0 76.9 jit_solution(14473028828297898942)
XLA Ops:
  0.7 75.0 %shard_map.55 = bf16[256,3072]{1,0:T(8,128)(2,1)S(1)} custom-call(s32[1]{0:T(128)S(6)} %copy.7.count_ref, s32[1,256]{1,0:T(1,128)} %bitcast.1, bf16[256,9216]{1,0:T(8,128)(2,1)} %fresh.1, bf16[256,6144]{1,0:T(8,128)(2,1)} %stale.1, bf16[256,3072]{1,0:T(8,128)(2,1)} %stale_out.1), custom_call_target="tpu_custom_call" | custom-call | flops 6442450944 | bytes 12582912 | tf_op jit(solution)/shard_map/pallas_call | solution.py:313
  75.7 1.1 %copy.8 = bf16[256,3072]{1,0:T(8,128)(2,1)} copy(bf16[256,3072]{1,0:T(8,128)(2,1)S(1)} %shard_map.55) | data formatting | bytes 3145728

commit v7 on v4

--- a/solution.py
+++ b/solution.py
@@ -233,20 +233,6 @@
             o_copy(j, peer(step)).start()
 
     def head(j, carry):
-        @pl.when(j > 0)
-        def _():
-            sent_kv(j)
-
-            @pl.when(j + 1 < heads_own)
-            def _():
-                send_kv(j + 1)
-
-            sent_q(j)
-
-            @pl.when(j + 1 < heads_own)
-            def _():
-                send_q(j + 1)
-
         @pl.when(j + 1 == heads_own)
         def _():
             def early(before, carry):
@@ -255,6 +241,20 @@
                 return carry
 
             lax.fori_loop(0, heads_own - 1, early, 0)
+
+        @pl.when(j > 0)
+        def _():
+            sent_kv(j)
+
+            @pl.when(j + 1 < heads_own)
+            def _():
+                send_kv(j + 1)
+
+            sent_q(j)
+
+            @pl.when(j + 1 < heads_own)
+            def _():
+                send_q(j + 1)
 
         for step in order:
             wait_kv(j, peer(step))

time: 76.9 us -> 77.6 us (level)
  no operation moved by 1% of the time
where the time goes in v7:
time: 77.6 us; the launch traced here: 76.9 us
  Pallas kernels  75 us (97%)
  local copies, waits for them, and re-layouts  1.15 us (1%)
    pallas_call x1, Pallas kernels, on_device(): pl.pallas_call(functools.partial(kernel, n, heads_own), out_shape=jax.Sha...  75 us

profile of v7, /device:TPU:64, one launch (start us, length us, event | category | flops | bytes accessed | tf_op | source)
XLA Modules:
  0.0 76.9 jit_solution(5736316939100473267)
XLA Ops:
  0.7 75.0 %shard_map.55 = bf16[256,3072]{1,0:T(8,128)(2,1)S(1)} custom-call(s32[1]{0:T(128)S(6)} %copy.7.count_ref, s32[1,256]{1,0:T(1,128)} %bitcast.1, bf16[256,9216]{1,0:T(8,128)(2,1)} %fresh.1, bf16[256,6144]{1,0:T(8,128)(2,1)} %stale.1, bf16[256,3072]{1,0:T(8,128)(2,1)} %stale_out.1), custom_call_target="tpu_custom_call" | custom-call | flops 6442450944 | bytes 12582912 | tf_op jit(solution)/shard_map/pallas_call | solution.py:306
  75.7 1.1 %copy.8 = bf16[256,3072]{1,0:T(8,128)(2,1)} copy(bf16[256,3072]{1,0:T(8,128)(2,1)S(1)} %shard_map.55) | data formatting | bytes 3145728
